TPU v7x, 32 devices: a whole 2x2x4 slice. The times are simulated.
32 devices in a mesh: patch: 16 (over z, y, core), head: 2 (over x).
Axes of the slice: x: 2, y: 2, z: 4, core: 2. Of those that a mesh axis runs over, the one named last changes fastest.
Arguments:
- fresh_q: bfloat16 [1536, 3072], P(('patch', 'head')), may hold values from -180 to 180
- fresh_k: bfloat16 [1536, 3072], P(('patch', 'head')), may hold values from -180 to 180
- fresh_v: bfloat16 [1536, 3072], P(('patch', 'head')), may hold values from -6 to 6
- stale_k: bfloat16 [1536, 3072], P('patch', 'head'), may hold values from -20 to 20
- stale_v: bfloat16 [1536, 3072], P('patch', 'head'), may hold values from -6 to 6
- q_gain: float32 [3072], replicated, may hold values from 0.1 to 1.9
- k_gain: float32 [3072], replicated, may hold values from 0.1 to 1.9
Outputs:
- attended: bfloat16 [1536, 3072], P(('patch', 'head'))
- key_cache: bfloat16 [1536, 3072], P('patch', 'head')
All inputs are finite; a program needn't handle non-finite values.
Results may differ from a plain program's by a relative error of at most 0.011.
Values may be sent and summed in bfloat16 or wider, within the bound.
A program may use at most 192 MiB of HBM per device.

v0:
```python
import jax
import jax.numpy as jnp
from jax import lax
from jax.sharding import PartitionSpec as P

HEADS = 24
HD = 128


EPSILON = 1e-06
LOWEST = -1e30


def scale_rows(source, square_sum, gain, width_all):
    values = source.astype(jnp.float32)
    factor = lax.rsqrt(square_sum[:, None] / width_all + EPSILON)
    return (values * factor * gain[None, :]).astype(jnp.bfloat16)


def heads_view(source, heads_dev):
    return source.reshape(source.shape[0], heads_dev, source.shape[1] // heads_dev)


def scaled_scores(queries, key_rows):
    score_scale = HD ** (-0.5)
    return (
        jnp.einsum("qhe,khe->hqk", queries, key_rows, preferred_element_type=jnp.float32)
        * score_scale
    )


def block_stats(scores, value_rows):
    row_max = jnp.max(scores, axis=2)
    weights = jnp.exp(scores - row_max[:, :, None])
    row_sum = jnp.sum(weights, axis=2)
    weighted = jnp.einsum(
        "hqk,khe->hqe", weights.astype(jnp.bfloat16), value_rows, preferred_element_type=jnp.float32
    )
    return (row_max, row_sum, weighted)


def absorb(carried, scores, value_rows):
    row_max, row_sum, weighted = carried
    new_max = jnp.maximum(row_max, jnp.max(scores, axis=2))
    rescale = jnp.exp(row_max - new_max)
    weights = jnp.exp(scores - new_max[:, :, None])
    row_sum = row_sum * rescale + jnp.sum(weights, axis=2)
    added = jnp.einsum(
        "hqk,khe->hqe", weights.astype(jnp.bfloat16), value_rows, preferred_element_type=jnp.float32
    )
    return (new_max, row_sum, weighted * rescale[:, :, None] + added)


def body(fresh_q, fresh_k, fresh_v, stale_k, stale_v, q_gain, k_gain):
    groups = lax.axis_size("head")
    heads_dev = HEADS // groups
    width_dev = heads_dev * HD
    width_all = q_gain.shape[0]
    local_q, local_k, local_v = (
        lax.all_to_all(fresh_q, "head", split_axis=1, concat_axis=0, tiled=True),
        lax.all_to_all(fresh_k, "head", split_axis=1, concat_axis=0, tiled=True),
        lax.all_to_all(fresh_v, "head", split_axis=1, concat_axis=0, tiled=True),
    )
    first_col = lax.axis_index("head") * width_dev
    gain_q = lax.dynamic_slice_in_dim(q_gain, first_col, width_dev, 0)
    gain_k = lax.dynamic_slice_in_dim(k_gain, first_col, width_dev, 0)
    squares_q = jnp.sum(jnp.square(local_q.astype(jnp.float32)), axis=1)
    squares_k = jnp.sum(jnp.square(local_k.astype(jnp.float32)), axis=1)
    total_q, total_k = lax.psum((squares_q, squares_k), "head")
    normed_q = scale_rows(local_q, total_q, gain_q, width_all)
    key_cache = scale_rows(local_k, total_k, gain_k, width_all)
    patch_rows = normed_q.shape[0]
    my_patch = lax.axis_index("patch")
    query_view = heads_view(normed_q, heads_dev)
    fresh_state = block_stats(
        scaled_scores(query_view, heads_view(key_cache, heads_dev)), heads_view(local_v, heads_dev)
    )
    segment = (
        lax.all_gather(stale_k, "patch", axis=0, tiled=True),
        lax.all_gather(stale_v, "patch", axis=0, tiled=True),
    )
    key_rows = heads_view(segment[0], heads_dev)
    value_rows = heads_view(segment[1], heads_dev)
    scores = scaled_scores(query_view, key_rows)
    owner_patch = jnp.arange(segment[0].shape[0], dtype=jnp.int32) // patch_rows
    scores = jnp.where((owner_patch == my_patch)[None, None, :], 2.0 * LOWEST, scores)
    folded = absorb(fresh_state, scores, value_rows)
    row_max, row_sum, weighted = folded
    result = (weighted / row_sum[:, :, None]).astype(jnp.bfloat16)
    result = jnp.transpose(result, (1, 0, 2)).reshape(patch_rows, width_dev)
    attended = lax.all_to_all(result, "head", split_axis=0, concat_axis=1, tiled=True)
    return (attended, key_cache)


def solution(mesh):
    placed = (
        P(("patch", "head"), None),
        P(("patch", "head"), None),
        P(("patch", "head"), None),
        P("patch", "head"),
        P("patch", "head"),
        P(),
        P(),
    )
    return jax.shard_map(
        body,
        mesh=mesh,
        in_specs=placed,
        out_specs=(P(("patch", "head"), None), P("patch", "head")),
        check_vma=False,
    )
```

profile of v0, /device:TPU:0, one launch (start us, length us, event | category | flops | bytes accessed | tf_op | source)
XLA Modules:
  0.0 152.2 jit_solution(5132674795662869103)
XLA Ops:
  7.2 0.0 copy-start
  7.2 0.0 all-gather.3.cloned.1.call-start
  7.2 0.7 all-gather.3.cloned.1.call-update
  7.9 0.0 all-gather.5.cloned.1.call-start
  8.0 0.7 all-gather.5.cloned.1.call-update
  8.7 1.7 %copy.78 = bf16[6,2,8,1536]{3,2,0,1:T(8,128)(2,1)} copy(bf16[6,2,8,1536]{3,2,1,0:T(8,128)(2,1)} %bitcast.65) | data formatting | bytes 589824 | tf_op jit(solution)/shard_map/all_to_all | solution.py:60
  10.4 4.2 %all-to-all-start = ((bf16[48,2,1536]{2,0,1:T(8,128)(2,1)}), bf16[48,2,1536]{2,0,1:T(8,128)(2,1)S(1)}, u32[]{:S(2)}, u32[]{:S(2)}) async-start(bf16[48,2,1536]{2,0,1:T(8,128)(2,1)} %bitcast.60), calls=%async_computation | async-start | bytes 589824 | tf_op jit(solution)/shard_map/all_to_all | solution.py:60
  14.6 0.8 dynamic-slice_bitcast_fusion.1
  15.4 0.8 dynamic_slice.7
  16.1 1.7 %copy.77 = bf16[6,2,8,1536]{3,2,0,1:T(8,128)(2,1)} copy(bf16[6,2,8,1536]{3,2,1,0:T(8,128)(2,1)} %bitcast.66) | data formatting | bytes 589824 | tf_op jit(solution)/shard_map/all_to_all | solution.py:61
  17.8 1.7 %copy.76 = bf16[6,2,8,1536]{3,2,0,1:T(8,128)(2,1)} copy(bf16[6,2,8,1536]{3,2,1,0:T(8,128)(2,1)} %bitcast.67) | data formatting | bytes 589824 | tf_op jit(solution)/shard_map/all_to_all | solution.py:62
  19.5 0.0 copy-done
  19.5 0.1 dynamic-slice_bitcast_fusion
  19.6 1.2 all-to-all-done
  20.8 3.5 %all-to-all-start.1 = ((bf16[48,2,1536]{2,0,1:T(8,128)(2,1)}), bf16[48,2,1536]{2,0,1:T(8,128)(2,1)S(1)}, u32[]{:S(2)}, u32[]{:S(2)}) async-start(bf16[48,2,1536]{2,0,1:T(8,128)(2,1)} %bitcast.59), calls=%async_computation.1 | async-start | bytes 589824 | tf_op jit(solution)/shard_map/all_to_all | solution.py:61
  24.3 5.3 %all-to-all-done.1 = bf16[48,2,1536]{2,0,1:T(8,128)(2,1)S(1)} async-done(((bf16[48,2,1536]{2,0,1:T(8,128)(2,1)}), bf16[48,2,1536]{2,0,1:T(8,128)(2,1)S(1)}, u32[]{:S(2)}, u32[]{:S(2)}) %all-to-all-start.1) | async-done | bytes 294944 | tf_op jit(solution)/shard_map/all_to_all | solution.py:61
  29.6 3.5 %all-to-all-start.2 = ((bf16[48,2,1536]{2,0,1:T(8,128)(2,1)}), bf16[48,2,1536]{2,0,1:T(8,128)(2,1)S(1)}, u32[]{:S(2)}, u32[]{:S(2)}) async-start(bf16[48,2,1536]{2,0,1:T(8,128)(2,1)} %bitcast.58), calls=%async_computation.2 | async-start | bytes 589824 | tf_op jit(solution)/shard_map/all_to_all | solution.py:62
  33.1 0.1 fusion.16
  33.2 0.1 reshape.109
  33.4 0.1 reduce_sum.50
  33.4 0.1 multiply_reduce_fusion
  33.6 0.1 reduce_sum.53
  33.7 0.1 reshape.110
  33.8 4.6 %all-to-all-done.2 = bf16[48,2,1536]{2,0,1:T(8,128)(2,1)S(1)} async-done(((bf16[48,2,1536]{2,0,1:T(8,128)(2,1)}), bf16[48,2,1536]{2,0,1:T(8,128)(2,1)S(1)}, u32[]{:S(2)}, u32[]{:S(2)}) %all-to-all-start.2) | async-done | bytes 294944 | tf_op jit(solution)/shard_map/all_to_all | solution.py:62
  38.4 0.2 reshape.106
  38.6 4.9 %all-reduce = (f32[96]{0:T(128)S(1)}, f32[96]{0:T(128)S(1)}) all-reduce(f32[96]{0:T(128)S(1)} %reduce_sum.50, f32[96]{0:T(128)S(1)} %reduce_sum.53), channel_id=1, replica_groups=mesh['patch'=16,'head'=2] {'head'}, use_global_device_ids=true, to_apply=%region_1.0 | all-reduce | flops 192 | bytes 1536 | tf_op jit(solution)/shard_map/psum | solution.py:69
  43.6 0.2 multiply_convert_fusion.1
  43.7 0.2 multiply_convert_fusion
  43.9 0.3 fusion.36
  44.3 0.1 fusion.19
  44.4 22.0 %all-gather.3.cloned.1.call-done = bf16[1536,1536]{1,0:T(8,128)(2,1)} async-done(((bf16[96,1536]{1,0:T(8,128)(2,1)}), bf16[1536,1536]{1,0:T(8,128)(2,1)}) %all-gather.3.cloned.1.call-update) | async-done | bytes 4718608 | tf_op jit(solution)/shard_map/all_gather | solution.py:79
  66.4 6.6 %copy.45 = bf16[1536,1536]{0,1:T(8,128)(2,1)} copy(bf16[1536,1536]{1,0:T(8,128)(2,1)} %all-gather.3.cloned.1.call-done) | data formatting | bytes 9437184 | tf_op jit(solution)/shard_map/all_gather | solution.py:79
  73.1 4.0 %fusion = (f32[12,96]{1,0:T(8,128)S(1)}, f32[12,96,1536]{2,1,0:T(8,128)S(1)}) fusion(pred[1536]{0:T(1024)(128)(4,1)S(1)} %fusion.28, bf16[1536,12,128]{0,2,1:T(8,128)(2,1)} %bitcast.61, bf16[96,12,128]{2,1,0:T(8,128)(2,1)S(1)} %multiply_convert_fusion.1), kind=kOutput, calls=%fused_computation.2 | convolution fusion | flops 458292096 | bytes 12097536 | tf_op jit(solution)/shard_map/qhe,khe->hqk/dot_general | solution.py:27
  77.1 0.0 copy-start.1
  77.1 2.9 %copy-done.1 = f32[12,96,1536]{2,1,0:T(8,128)} copy-done((f32[12,96,1536]{2,1,0:T(8,128)}, f32[12,96,1536]{2,1,0:T(8,128)S(1)}, u32[]{:S(2)}) %copy-start.1) | copy-done | bytes 7077912
  80.0 1.6 %fusion.1 = f32[12,96]{1,0:T(8,128)S(1)} fusion(f32[12,96,1536]{2,1,0:T(8,128)S(1)} %get-tuple-element.9, f32[12,96]{1,0:T(8,128)S(1)} %max.18, pred[1536]{0:T(1024)(128)(4,1)S(1)} %fusion.28), kind=kLoop, calls=%fused_computation.3 | loop fusion | flops 7076736 | bytes 7088640 | tf_op jit(solution)/shard_map/reduce_sum | solution.py:47
  81.7 39.0 %all-gather.5.cloned.1.call-done = bf16[1536,1536]{1,0:T(8,128)(2,1)} async-done(((bf16[96,1536]{1,0:T(8,128)(2,1)}), bf16[1536,1536]{1,0:T(8,128)(2,1)}) %all-gather.5.cloned.1.call-update) | async-done | bytes 4718608 | tf_op jit(solution)/shard_map/all_gather | solution.py:80
  120.7 6.6 %copy.48 = bf16[1536,1536]{0,1:T(8,128)(2,1)} copy(bf16[1536,1536]{1,0:T(8,128)(2,1)} %all-gather.5.cloned.1.call-done) | data formatting | bytes 9437184 | tf_op jit(solution)/shard_map/all_gather | solution.py:80
  127.3 6.1 %fusion.9 = f32[96,12,128]{2,0,1:T(8,128)S(1)} fusion(bf16[1536,12,128]{0,2,1:T(8,128)(2,1)} %bitcast.62, f32[12,96,1536]{2,1,0:T(8,128)} %copy-done.1, f32[12,96]{1,0:T(8,128)S(1)} %max.18, pred[1536]{0:T(1024)(128)(4,1)S(1)} %fusion.28), kind=kOutput, calls=%fused_computation.10 | convolution fusion | flops 460062720 | bytes 12392448 | tf_op jit(solution)/shard_map/hqk,khe->hqe/dot_general | solution.py:48
  133.4 0.5 fusion.15
  133.9 0.1 copy.50
  134.1 0.9 all_to_all.53
  135.0 3.4 %all-to-all-start.3 = ((bf16[2,48,1536]{2,1,0:T(8,128)(2,1)}), bf16[2,48,1536]{2,1,0:T(8,128)(2,1)S(1)}, u32[]{:S(2)}, u32[]{:S(2)}) async-start(bf16[2,48,1536]{2,1,0:T(8,128)(2,1)} %all_to_all.53), calls=%async_computation.3 | async-start | bytes 589824 | tf_op jit(solution)/shard_map/all_to_all | solution.py:91
  138.5 0.9 fusion.18
  139.3 5.4 %all-to-all-done.3 = bf16[2,48,1536]{2,1,0:T(8,128)(2,1)S(1)} async-done(((bf16[2,48,1536]{2,1,0:T(8,128)(2,1)}), bf16[2,48,1536]{2,1,0:T(8,128)(2,1)S(1)}, u32[]{:S(2)}, u32[]{:S(2)}) %all-to-all-start.3) | async-done | bytes 294944 | tf_op jit(solution)/shard_map/all_to_all | solution.py:91
  144.7 0.7 copy.58
  (7 shorter events, 0.1 us)
Async XLA Ops:
  7.2 12.4 %copy-start = (f32[3072]{0:T(1024)S(1)}, f32[3072]{0:T(1024)}, u32[]{:S(2)}) copy-start(f32[3072]{0:T(1024)} %param.12) | copy-start | bytes 36868
  7.2 59.2 %all-gather.3.cloned.1.call-start = ((), (), s32[]{:S(2)}) async-start(), calls=%async_computation.4 | async-start | bytes 5013504 | tf_op jit(solution)/shard_map/all_gather | solution.py:79
  7.9 112.8 %all-gather.5.cloned.1.call-start = ((), (), s32[]{:S(2)}) async-start(), calls=%async_computation.5 | async-start | bytes 5013504 | tf_op jit(solution)/shard_map/all_gather | solution.py:80
  10.4 10.4 %all-to-all-start = ((bf16[48,2,1536]{2,0,1:T(8,128)(2,1)}), bf16[48,2,1536]{2,0,1:T(8,128)(2,1)S(1)}, u32[]{:S(2)}, u32[]{:S(2)}) async-start(bf16[48,2,1536]{2,0,1:T(8,128)(2,1)} %bitcast.60), calls=%async_computation | async-start | bytes 589824 | tf_op jit(solution)/shard_map/all_to_all | solution.py:60
  20.8 8.8 %all-to-all-start.1 = ((bf16[48,2,1536]{2,0,1:T(8,128)(2,1)}), bf16[48,2,1536]{2,0,1:T(8,128)(2,1)S(1)}, u32[]{:S(2)}, u32[]{:S(2)}) async-start(bf16[48,2,1536]{2,0,1:T(8,128)(2,1)} %bitcast.59), calls=%async_computation.1 | async-start | bytes 589824 | tf_op jit(solution)/shard_map/all_to_all | solution.py:61
  29.6 8.8 %all-to-all-start.2 = ((bf16[48,2,1536]{2,0,1:T(8,128)(2,1)}), bf16[48,2,1536]{2,0,1:T(8,128)(2,1)S(1)}, u32[]{:S(2)}, u32[]{:S(2)}) async-start(bf16[48,2,1536]{2,0,1:T(8,128)(2,1)} %bitcast.58), calls=%async_computation.2 | async-start | bytes 589824 | tf_op jit(solution)/shard_map/all_to_all | solution.py:62
  77.1 2.9 %copy-start.1 = (f32[12,96,1536]{2,1,0:T(8,128)}, f32[12,96,1536]{2,1,0:T(8,128)S(1)}, u32[]{:S(2)}) copy-start(f32[12,96,1536]{2,1,0:T(8,128)S(1)} %get-tuple-element.9) | copy-start | bytes 21233668
  135.0 9.7 %all-to-all-start.3 = ((bf16[2,48,1536]{2,1,0:T(8,128)(2,1)}), bf16[2,48,1536]{2,1,0:T(8,128)(2,1)S(1)}, u32[]{:S(2)}, u32[]{:S(2)}) async-start(bf16[2,48,1536]{2,1,0:T(8,128)(2,1)} %all_to_all.53), calls=%async_computation.3 | async-start | bytes 589824 | tf_op jit(solution)/shard_map/all_to_all | solution.py:91
Sparse Core Ops, SparseCore 0:
  10.3 56.0 all-gather.2
  68.7 51.9 all-gather.4
where the time goes:
time: 153 us; the launch traced here: 152 us
  waiting for transfers between devices  78.8 us (52%)
  local copies, waits for them, and re-layouts  25.3 us (17%)
  starting transfers between devices  14.6 us (10%)
  between operations  14.2 us (9%)
  matrix products  11 us (7%)
  blocking collectives  4.94 us (3%)
  other arithmetic  3.38 us (2%)
    all_gather x1, waiting for transfers between devices, body(): lax.all_gather(stale_v, 'patch', axis=0, tiled=True)  39 us
    all_gather x1, waiting for transfers between devices, body(): lax.all_gather(stale_k, 'patch', axis=0, tiled=True)  22 us
    all_gather x1, local copies, waits for them, and re-layouts, body(): lax.all_gather(stale_k, 'patch', axis=0, tiled=True)  6.64 us
    all_gather x1, local copies, waits for them, and re-layouts, body(): lax.all_gather(stale_v, 'patch', axis=0, tiled=True)  6.64 us
    dot_general x1, matrix products, absorb(): jnp.einsum('hqk,khe->hqe', weights.astype(jnp.bfloat16), value_rows, pref...  6.09 us
    all_to_all x1, waiting for transfers between devices, body(): lax.all_to_all(result, 'head', split_axis=0, concat_axis=1, tiled=True)  5.35 us
    all_to_all x1, waiting for transfers between devices, body(): lax.all_to_all(fresh_k, 'head', split_axis=1, concat_axis=0, tiled=True)  5.28 us
    psum x1, blocking collectives, body(): total_q, total_k = lax.psum((squares_q, squares_k), 'head')  4.94 us
  transfers between devices with their start and end apart: 6, of which 6 were waited for; matrix products, arithmetic and copies ran while one was open for 14% of the time, Pallas kernels for 0%

commit v1 on v0

--- a/solution.py
+++ b/solution.py
@@ -1,6 +1,8 @@
 import jax
 import jax.numpy as jnp
 from jax import lax
+from jax.experimental import pallas as pl
+from jax.experimental.pallas import tpu as pltpu
 from jax.sharding import PartitionSpec as P
 
 HEADS = 24
@@ -91,6 +93,265 @@
     attended = lax.all_to_all(result, "head", split_axis=0, concat_axis=1, tiled=True)
     return (attended, key_cache)
 
+SPLIT = 4
+MESH_TYPE = pl.DeviceIdType.MESH
+
+
+def rms_rows(source, gain):
+    values = source.astype(jnp.float32)
+    mean_square = jnp.mean(values * values, axis=1, keepdims=True)
+    return (values * lax.rsqrt(mean_square + EPSILON) * gain).astype(jnp.bfloat16)
+
+
+def kernel(
+    fresh_q, fresh_k, fresh_v, stale_k, stale_v, q_gain, k_gain,
+    attended, key_cache,
+    normed_q, normed_k, q_rows, fresh_k_rows, fresh_v_rows, k_rows, v_rows, result,
+    fresh_send, fresh_recv, stale_send, stale_recv, pass_send, pass_recv,
+    out_send, out_recv, cache_send, cache_recv, local_sem,
+):
+    half_rows = fresh_q.shape[0]
+    patch_rows, width_dev = stale_k.shape
+    width = width_dev // SPLIT
+    heads = width // HD
+    chunk = SPLIT * patch_rows
+
+    patch, x = lax.axis_index("patch"), lax.axis_index("head")
+    core, y = lax.rem(patch, 2), lax.rem(patch // 2, 2)
+    low, high = lax.rem(patch // 4, 2), patch // 8
+
+    def flip(bit, by):
+        return lax.rem(bit + by, 2)
+
+    def patch_at(by_high, by_low, by_y, by_core=0):
+        return flip(high, by_high) * 8 + flip(low, by_low) * 4 + flip(y, by_y) * 2 + flip(core, by_core)
+
+    def group_at(by_low, by_y):
+        return flip(low, by_low) * 2 + flip(y, by_y)
+
+    def rows_of(index, size):
+        return pl.ds(pl.multiple_of(index * size, size), size)
+
+    def columns_of(index):
+        return pl.ds(pl.multiple_of(index * width, width), width)
+
+    cube = [(dx, dl, dy) for dx in range(2) for dl in range(2) for dy in range(2)]
+    plane = [(dh, dl, dy) for dh in range(2) for dl in range(2) for dy in range(2)]
+    sibling = (patch_at(0, 0, 0, 1), x)
+
+    barrier = pltpu.get_barrier_semaphore()
+    partners = [(patch_at(0, dl, dy), flip(x, dx)) for dx, dl, dy in cube[1:]]
+    partners += [(patch_at(1, dl, dy), x) for dh, dl, dy in plane[4:]]
+    partners += [sibling]
+    for partner in partners:
+        pl.semaphore_signal(barrier, inc=1, device_id=partner, device_id_type=MESH_TYPE)
+
+    normed_q[...] = rms_rows(fresh_q[...], q_gain[...])
+    normed_k[...] = rms_rows(fresh_k[...], k_gain[...])
+    pl.semaphore_wait(barrier, len(partners))
+
+    started, local = [], []
+
+    def send(source, target, send_sem, recv_sem, device):
+        copy = pltpu.make_async_remote_copy(
+            src_ref=source, dst_ref=target, send_sem=send_sem, recv_sem=recv_sem,
+            device_id=device, device_id_type=MESH_TYPE,
+        )
+        copy.start()
+        started.append(copy)
+
+    def arrive(target, send_sem, recv_sem, device):
+        pltpu.make_async_remote_copy(
+            src_ref=target, dst_ref=target, send_sem=send_sem, recv_sem=recv_sem,
+            device_id=device, device_id_type=MESH_TYPE,
+        ).wait_recv()
+
+    def place(source, target):
+        copy = pltpu.make_async_copy(source, target, local_sem.at[len(local)])
+        copy.start()
+        local.append(copy)
+        return copy
+
+    my_rows = rows_of(group_at(0, 0) * 2 + x, half_rows)
+    my_columns = columns_of(x * SPLIT + group_at(0, 0))
+    fresh = [(normed_q, q_rows), (normed_k, fresh_k_rows), (fresh_v, fresh_v_rows)]
+    stale = [(stale_k, k_rows), (stale_v, v_rows)]
+
+    def send_fresh(t):
+        source, target = fresh[t]
+        for i, (dx, dl, dy) in enumerate(cube):
+            columns = columns_of(flip(x, dx) * SPLIT + group_at(dl, dy))
+            if i == 0:
+                place(source.at[:, columns], target.at[my_rows])
+            else:
+                send(
+                    source.at[:, columns], target.at[my_rows],
+                    fresh_send.at[t, i], fresh_recv.at[t, i],
+                    (patch_at(0, dl, dy), flip(x, dx)),
+                )
+
+    def send_stale(i):
+        dh, dl, dy = plane[i]
+        rows = rows_of(patch, patch_rows)
+        for t, (source, target) in enumerate(stale):
+            block = source.at[:, columns_of(group_at(dl, dy))]
+            if i == 0:
+                place(block, target.at[rows])
+                send(block, target.at[rows], pass_send.at[t, 0], pass_recv.at[t, 0], sibling)
+            else:
+                send(
+                    block, target.at[rows], stale_send.at[t, i], stale_recv.at[t, i],
+                    (patch_at(dh, dl, dy), x),
+                )
+
+    send_fresh(0)
+    for i in range(4, 8):
+        send_stale(i)
+    send_fresh(1)
+    send_fresh(2)
+    for i in range(4):
+        send_stale(i)
+    cache_rows = rows_of(x, half_rows)
+    side = pl.ds(pl.multiple_of(x * width_dev, width_dev), width_dev)
+    other_side = pl.ds(pl.multiple_of((1 - x) * width_dev, width_dev), width_dev)
+    place(normed_k.at[:, side], key_cache.at[cache_rows])
+    send(
+        normed_k.at[:, other_side], key_cache.at[cache_rows],
+        cache_send.at[0], cache_recv.at[0], (patch, 1 - x),
+    )
+    for copy in local:
+        copy.wait()
+
+    for t, (_, target) in enumerate(fresh):
+        for i, (dx, dl, dy) in enumerate(cube):
+            if i > 0:
+                arrive(
+                    target.at[rows_of(group_at(dl, dy) * 2 + flip(x, dx), half_rows)],
+                    fresh_send.at[t, i], fresh_recv.at[t, i],
+                    (patch_at(0, dl, dy), flip(x, dx)),
+                )
+
+    factor = HD ** (-0.5) * 1.4426950408889634
+    state = [None] * heads
+    row_patch = lax.broadcasted_iota(jnp.int32, (chunk, 1), 0) // patch_rows
+    column_patch = lax.broadcasted_iota(jnp.int32, (1, chunk), 1) // patch_rows
+
+    def attend(h, keys, values, masked):
+        columns = slice(h * HD, (h + 1) * HD)
+        scores = lax.dot_general(
+            q_rows[:, columns], keys[:, columns], (((1,), (1,)), ((), ())),
+            preferred_element_type=jnp.float32,
+        )
+        if masked is not None:
+            scores = jnp.where(masked, 2.0 * LOWEST, scores)
+        new_max = jnp.max(scores, axis=1, keepdims=True)
+        if state[h] is not None:
+            row_max, row_sum, weighted = state[h]
+            new_max = jnp.maximum(row_max, new_max)
+        weights = jnp.exp2((scores - new_max) * factor)
+        new_sum = jnp.sum(weights, axis=1, keepdims=True)
+        added = jnp.dot(
+            weights.astype(jnp.bfloat16), values[:, columns], preferred_element_type=jnp.float32
+        )
+        if state[h] is not None:
+            rescale = jnp.exp2((row_max - new_max) * factor)
+            new_sum += row_sum * rescale
+            added += weighted * rescale
+        state[h] = (new_max, new_sum, added)
+
+    for h in range(heads):
+        attend(h, fresh_k_rows, fresh_v_rows, row_patch != column_patch)
+
+    for dh, dl in ((0, 0), (0, 1), (1, 0), (1, 1)):
+        indices = [i for i in range(8) if plane[i][:2] == (dh, dl)]
+        for i in indices:
+            rows = rows_of(patch_at(*plane[i]), patch_rows)
+            for t, (_, target) in enumerate(stale):
+                if i > 0:
+                    arrive(
+                        target.at[rows], stale_send.at[t, i], stale_recv.at[t, i],
+                        (patch_at(*plane[i]), x),
+                    )
+                    send(
+                        target.at[rows], target.at[rows],
+                        pass_send.at[t, i], pass_recv.at[t, i], sibling,
+                    )
+        for i in indices:
+            rows = rows_of(patch_at(*plane[i], 1), patch_rows)
+            for t, (_, target) in enumerate(stale):
+                arrive(target.at[rows], pass_send.at[t, i], pass_recv.at[t, i], sibling)
+        block = rows_of(flip(high, dh) * 2 + flip(low, dl), chunk)
+        masked = None
+        if dh == 0:
+            key_patch = column_patch + flip(low, dl) * 4
+            masked = row_patch * 2 + core == key_patch
+        for h in range(heads):
+            attend(h, k_rows.at[block], v_rows.at[block], masked)
+
+    for h in range(heads):
+        _, row_sum, weighted = state[h]
+        result[:, h * HD : (h + 1) * HD] = (weighted / row_sum).astype(jnp.bfloat16)
+
+    last = None
+    for i, (dx, dl, dy) in enumerate(cube):
+        rows = rows_of(group_at(dl, dy) * 2 + flip(x, dx), half_rows)
+        if i == 0:
+            last = place(result.at[rows], attended.at[:, my_columns])
+        else:
+            send(
+                result.at[rows], attended.at[:, my_columns], out_send.at[i], out_recv.at[i],
+                (patch_at(0, dl, dy), flip(x, dx)),
+            )
+    arrive(key_cache.at[rows_of(1 - x, half_rows)], cache_send.at[0], cache_recv.at[0], (patch, 1 - x))
+    for i, (dx, dl, dy) in enumerate(cube):
+        if i > 0:
+            arrive(
+                attended.at[:, columns_of(flip(x, dx) * SPLIT + group_at(dl, dy))],
+                out_send.at[i], out_recv.at[i], (patch_at(0, dl, dy), flip(x, dx)),
+            )
+    last.wait()
+    for copy in started:
+        copy.wait_send()
+
+
+def kernel_body(fresh_q, fresh_k, fresh_v, stale_k, stale_v, q_gain, k_gain):
+    half_rows, width_all = fresh_q.shape
+    patch_rows, width_dev = stale_k.shape
+    tokens = patch_rows * lax.axis_size("patch")
+    width = width_dev // SPLIT
+    group = (SPLIT * patch_rows, width)
+    bf16 = jnp.bfloat16
+    in_vmem = pl.BlockSpec(memory_space=pltpu.VMEM)
+    anywhere = pl.BlockSpec(memory_space=pl.ANY)
+    sems = [(3, 8), (3, 8), (2, 8), (2, 8), (2, 8), (2, 8), (8,), (8,), (1,), (1,), (7,)]
+    pairs = (width_dev // HD) * patch_rows * tokens
+    return pl.pallas_call(
+        kernel,
+        out_shape=[
+            jax.ShapeDtypeStruct((half_rows, width_all), bf16),
+            jax.ShapeDtypeStruct((patch_rows, width_dev), bf16),
+        ],
+        in_specs=[in_vmem, in_vmem, anywhere, anywhere, anywhere, in_vmem, in_vmem],
+        out_specs=[anywhere, anywhere],
+        scratch_shapes=[
+            pltpu.VMEM((half_rows, width_all), bf16),
+            pltpu.VMEM((half_rows, width_all), bf16),
+            pltpu.VMEM(group, bf16),
+            pltpu.VMEM(group, bf16),
+            pltpu.VMEM(group, bf16),
+            pltpu.VMEM((tokens, width), bf16),
+            pltpu.VMEM((tokens, width), bf16),
+            pltpu.VMEM(group, bf16),
+        ]
+        + [pltpu.SemaphoreType.DMA(shape) for shape in sems],
+        compiler_params=pltpu.CompilerParams(
+            collective_id=0, has_side_effects=True, vmem_limit_bytes=40 * 1024 * 1024
+        ),
+        cost_estimate=pl.CostEstimate(
+            flops=4 * pairs * HD, bytes_accessed=8 * tokens * width, transcendentals=pairs
+        ),
+    )(fresh_q, fresh_k, fresh_v, stale_k, stale_v, q_gain[None, :], k_gain[None, :])
+
 
 def solution(mesh):
     placed = (
@@ -102,8 +363,9 @@
         P(),
         P(),
     )
+    fits = mesh.shape["patch"] == 16 and mesh.shape["head"] == 2
     return jax.shard_map(
-        body,
+        kernel_body if fits else body,
         mesh=mesh,
         in_specs=placed,
         out_specs=(P(("patch", "head"), None), P("patch", "head")),

time: 153 us -> 59.1 us (0.39)
  waiting for transfers between devices: 78.8 us -> 0 us
  Pallas kernels: 0 us -> 50.4 us
  local copies, waits for them, and re-layouts: 25.3 us -> 7.64 us
  starting transfers between devices: 14.6 us -> 0 us
  between operations: 14.2 us -> 0.66 us
  matrix products: 11 us -> 0 us
  blocking collectives: 4.94 us -> 0 us
  other arithmetic: 3.38 us -> 0 us
    all_gather x2 -> x0, waiting for transfers between devices: 61 us -> none  [the longest x1 39 us: body(): lax.all_gather(stale_v, 'patch', axis=0, tiled=True)]
    pallas_call x0 -> x1, Pallas kernels: none -> 50.4 us  [kernel_body(): pl.pallas_call(kernel, out_shape=[jax.ShapeDtypeStruct((half_rows, width_...]
    all_to_all x4 -> x0, waiting for transfers between devices: 16.4 us -> none  [the longest x1 5.35 us: body(): lax.all_to_all(result, 'head', split_axis=0, concat_axis=1, tiled=True)]
    all_to_all x4 -> x0, starting transfers between devices: 14.6 us -> none  [the longest x1 4.21 us: body(): lax.all_to_all(fresh_q, 'head', split_axis=1, concat_axis=0, tiled=True)]
    all_gather x2 -> x0, local copies, waits for them, and re-layouts: 13.3 us -> none  [the longest x1 6.64 us: body(): lax.all_gather(stale_k, 'patch', axis=0, tiled=True)]
    dot_general x4 -> x0, matrix products: 11 us -> none  [the longest x1 6.09 us: absorb(): jnp.einsum('hqk,khe->hqe', weights.astype(jnp.bfloat16), value_rows, pref...]
    all_to_all x5 -> x0, local copies, waits for them, and re-layouts: 6.73 us -> none  [the longest x1 1.69 us: body(): lax.all_to_all(fresh_q, 'head', split_axis=1, concat_axis=0, tiled=True)]
    psum x1 -> x0, blocking collectives: 4.94 us -> none  [body(): total_q, total_k = lax.psum((squares_q, squares_k), 'head')]
  transfers between devices with their start and end apart: 6 -> 0, of which waited for: 6 -> 0; matrix products, arithmetic and copies ran while one was open for 14% -> 0% of each run, Pallas kernels for 0% -> 0%
where the time goes in v1:
time: 59.1 us; the launch traced here: 58.7 us
  Pallas kernels  50.4 us (85%)
  local copies, waits for them, and re-layouts  7.64 us (13%)
  between operations  0.66 us (1%)
    pallas_call x1, Pallas kernels, kernel_body(): pl.pallas_call(kernel, out_shape=[jax.ShapeDtypeStruct((half_rows, width_...  50.4 us
    unnamed x16, local copies, waits for them, and re-layouts  7.64 us

profile of v1, /device:TPU:0, one launch (start us, length us, event | category | flops | bytes accessed | tf_op | source)
XLA Modules:
  0.0 58.7 jit_solution(4145694365490158280)
XLA Ops:
  0.6 0.0 copy-start
  0.6 1.0 %copy-done = bf16[48,3072]{1,0:T(8,128)(2,1)S(1)} copy-done((bf16[48,3072]{1,0:T(8,128)(2,1)S(1)}, bf16[48,3072]{1,0:T(8,128)(2,1)}, u32[]{:S(2)}) %copy-start) | copy-done | bytes 294936
  1.6 0.0 copy-start.1
  1.6 1.0 %copy-done.1 = bf16[48,3072]{1,0:T(8,128)(2,1)S(1)} copy-done((bf16[48,3072]{1,0:T(8,128)(2,1)S(1)}, bf16[48,3072]{1,0:T(8,128)(2,1)}, u32[]{:S(2)}) %copy-start.1) | copy-done | bytes 294936
  2.6 0.0 copy-start.2
  2.6 1.0 %copy-done.2 = bf16[48,3072]{1,0:T(8,128)(2,1)S(1)} copy-done((bf16[48,3072]{1,0:T(8,128)(2,1)S(1)}, bf16[48,3072]{1,0:T(8,128)(2,1)}, u32[]{:S(2)}) %copy-start.2) | copy-done | bytes 294936
  3.5 0.0 copy-start.3
  3.5 1.0 %copy-done.3 = bf16[96,1536]{1,0:T(8,128)(2,1)S(1)} copy-done((bf16[96,1536]{1,0:T(8,128)(2,1)S(1)}, bf16[96,1536]{1,0:T(8,128)(2,1)}, u32[]{:S(2)}) %copy-start.3) | copy-done | bytes 294936
  4.5 0.0 copy-start.4
  4.5 1.0 %copy-done.4 = bf16[96,1536]{1,0:T(8,128)(2,1)S(1)} copy-done((bf16[96,1536]{1,0:T(8,128)(2,1)S(1)}, bf16[96,1536]{1,0:T(8,128)(2,1)}, u32[]{:S(2)}) %copy-start.4) | copy-done | bytes 294936
  5.4 0.0 copy-start.5
  5.4 0.7 %copy-done.5 = f32[3072]{0:T(1024)S(1)} copy-done((f32[3072]{0:T(1024)S(1)}, f32[3072]{0:T(1024)}, u32[]{:S(2)}) %copy-start.5) | copy-done | bytes 12312
  6.2 0.0 copy-start.6
  6.2 0.7 %copy-done.6 = f32[3072]{0:T(1024)S(1)} copy-done((f32[3072]{0:T(1024)S(1)}, f32[3072]{0:T(1024)}, u32[]{:S(2)}) %copy-start.6) | copy-done | bytes 12312
  6.9 50.4 %shard_map.86 = (bf16[48,3072]{1,0:T(8,128)(2,1)S(1)}, bf16[96,1536]{1,0:T(8,128)(2,1)S(1)}) custom-call(bf16[48,3072]{1,0:T(8,128)(2,1)S(1)} %copy-done, bf16[48,3072]{1,0:T(8,128)(2,1)S(1)} %copy-done.1, bf16[48,3072]{1,0:T(8,128)(2,1)S(1)} %copy-done.2, bf16[96,1536]{1,0:T(8,128)(2,1)S(1)} %copy-done.3, bf16[96,1536]{1,0:T(8,128)(2,1)S(1)} %copy-done.4, ...), custom_call_target="tpu_custom_call" | custom-call | flops 905969664 | bytes 4718592 | tf_op jit(solution)/shard_map/pallas_call | solution.py:328
  57.3 0.7 %copy.11 = bf16[48,3072]{1,0:T(8,128)(2,1)} copy(bf16[48,3072]{1,0:T(8,128)(2,1)S(1)} %get-tuple-element.4) | data formatting | bytes 589824
  58.0 0.7 %copy.12 = bf16[96,1536]{1,0:T(8,128)(2,1)} copy(bf16[96,1536]{1,0:T(8,128)(2,1)S(1)} %get-tuple-element.5) | data formatting | bytes 589824
Async XLA Ops:
  0.6 1.0 %copy-start = (bf16[48,3072]{1,0:T(8,128)(2,1)S(1)}, bf16[48,3072]{1,0:T(8,128)(2,1)}, u32[]{:S(2)}) copy-start(bf16[48,3072]{1,0:T(8,128)(2,1)} %fresh_q.1) | copy-start | bytes 884740
  1.6 1.0 %copy-start.1 = (bf16[48,3072]{1,0:T(8,128)(2,1)S(1)}, bf16[48,3072]{1,0:T(8,128)(2,1)}, u32[]{:S(2)}) copy-start(bf16[48,3072]{1,0:T(8,128)(2,1)} %fresh_k.1) | copy-start | bytes 884740
  2.6 1.0 %copy-start.2 = (bf16[48,3072]{1,0:T(8,128)(2,1)S(1)}, bf16[48,3072]{1,0:T(8,128)(2,1)}, u32[]{:S(2)}) copy-start(bf16[48,3072]{1,0:T(8,128)(2,1)} %fresh_v.1) | copy-start | bytes 884740
  3.5 1.0 %copy-start.3 = (bf16[96,1536]{1,0:T(8,128)(2,1)S(1)}, bf16[96,1536]{1,0:T(8,128)(2,1)}, u32[]{:S(2)}) copy-start(bf16[96,1536]{1,0:T(8,128)(2,1)} %stale_k.1) | copy-start | bytes 884740
  4.5 1.0 %copy-start.4 = (bf16[96,1536]{1,0:T(8,128)(2,1)S(1)}, bf16[96,1536]{1,0:T(8,128)(2,1)}, u32[]{:S(2)}) copy-start(bf16[96,1536]{1,0:T(8,128)(2,1)} %stale_v.1) | copy-start | bytes 884740
  5.4 0.7 %copy-start.5 = (f32[3072]{0:T(1024)S(1)}, f32[3072]{0:T(1024)}, u32[]{:S(2)}) copy-start(f32[3072]{0:T(1024)} %param.12) | copy-start | bytes 36868
  6.2 0.7 %copy-start.6 = (f32[3072]{0:T(1024)S(1)}, f32[3072]{0:T(1024)}, u32[]{:S(2)}) copy-start(f32[3072]{0:T(1024)} %param.13) | copy-start | bytes 36868

commit v2 on v1

--- a/solution.py
+++ b/solution.py
@@ -106,7 +106,7 @@
 def kernel(
     fresh_q, fresh_k, fresh_v, stale_k, stale_v, q_gain, k_gain,
     attended, key_cache,
-    normed_q, normed_k, q_rows, fresh_k_rows, fresh_v_rows, k_rows, v_rows, result,
+    raw_q, raw_k, gains, normed_q, normed_k, q_rows, fresh_k_rows, fresh_v_rows, k_rows, v_rows, result,
     fresh_send, fresh_recv, stale_send, stale_recv, pass_send, pass_recv,
     out_send, out_recv, cache_send, cache_recv, local_sem,
 ):
@@ -135,6 +135,10 @@
     def columns_of(index):
         return pl.ds(pl.multiple_of(index * width, width), width)
 
+    def head_columns(dx, dl, dy, h):
+        first = (flip(x, dx) * SPLIT + group_at(dl, dy)) * width + h * HD
+        return pl.ds(pl.multiple_of(first, HD), HD)
+
     cube = [(dx, dl, dy) for dx in range(2) for dl in range(2) for dy in range(2)]
     plane = [(dh, dl, dy) for dh in range(2) for dl in range(2) for dy in range(2)]
     sibling = (patch_at(0, 0, 0, 1), x)
@@ -145,10 +149,6 @@
     partners += [sibling]
     for partner in partners:
         pl.semaphore_signal(barrier, inc=1, device_id=partner, device_id_type=MESH_TYPE)
-
-    normed_q[...] = rms_rows(fresh_q[...], q_gain[...])
-    normed_k[...] = rms_rows(fresh_k[...], k_gain[...])
-    pl.semaphore_wait(barrier, len(partners))
 
     started, local = [], []
 
@@ -172,8 +172,13 @@
         local.append(copy)
         return copy
 
+    place(fresh_q, raw_q)
+    place(fresh_k, raw_k)
+    place(q_gain, gains.at[0])
+    place(k_gain, gains.at[1])
+    pl.semaphore_wait(barrier, len(partners))
+
     my_rows = rows_of(group_at(0, 0) * 2 + x, half_rows)
-    my_columns = columns_of(x * SPLIT + group_at(0, 0))
     fresh = [(normed_q, q_rows), (normed_k, fresh_k_rows), (fresh_v, fresh_v_rows)]
     stale = [(stale_k, k_rows), (stale_v, v_rows)]
 
@@ -204,11 +209,15 @@
                     (patch_at(dh, dl, dy), x),
                 )
 
-    send_fresh(0)
     for i in range(4, 8):
         send_stale(i)
+    send_fresh(2)
+    for copy in local[:4]:
+        copy.wait()
+    normed_q[...] = rms_rows(raw_q[...], gains[0])
+    send_fresh(0)
+    normed_k[...] = rms_rows(raw_k[...], gains[1])
     send_fresh(1)
-    send_fresh(2)
     for i in range(4):
         send_stale(i)
     cache_rows = rows_of(x, half_rows)
@@ -219,7 +228,7 @@
         normed_k.at[:, other_side], key_cache.at[cache_rows],
         cache_send.at[0], cache_recv.at[0], (patch, 1 - x),
     )
-    for copy in local:
+    for copy in local[4:]:
         copy.wait()
 
     for t, (_, target) in enumerate(fresh):
@@ -259,10 +268,25 @@
             added += weighted * rescale
         state[h] = (new_max, new_sum, added)
 
+    def give_back(h):
+        _, row_sum, weighted = state[h]
+        columns = slice(h * HD, (h + 1) * HD)
+        result[:, columns] = (weighted / row_sum).astype(jnp.bfloat16)
+        for i, (dx, dl, dy) in enumerate(cube):
+            block = result.at[rows_of(group_at(dl, dy) * 2 + flip(x, dx), half_rows), columns]
+            target = attended.at[:, head_columns(0, 0, 0, h)]
+            if i == 0:
+                place(block, target)
+            else:
+                send(
+                    block, target, out_send.at[h, i], out_recv.at[h, i],
+                    (patch_at(0, dl, dy), flip(x, dx)),
+                )
+
     for h in range(heads):
         attend(h, fresh_k_rows, fresh_v_rows, row_patch != column_patch)
 
-    for dh, dl in ((0, 0), (0, 1), (1, 0), (1, 1)):
+    for dh, dl in ((1, 0), (1, 1), (0, 0), (0, 1)):
         indices = [i for i in range(8) if plane[i][:2] == (dh, dl)]
         for i in indices:
             rows = rows_of(patch_at(*plane[i]), patch_rows)
@@ -287,29 +311,19 @@
             masked = row_patch * 2 + core == key_patch
         for h in range(heads):
             attend(h, k_rows.at[block], v_rows.at[block], masked)
-
+            if (dh, dl) == (0, 1):
+                give_back(h)
+
+    arrive(key_cache.at[rows_of(1 - x, half_rows)], cache_send.at[0], cache_recv.at[0], (patch, 1 - x))
     for h in range(heads):
-        _, row_sum, weighted = state[h]
-        result[:, h * HD : (h + 1) * HD] = (weighted / row_sum).astype(jnp.bfloat16)
-
-    last = None
-    for i, (dx, dl, dy) in enumerate(cube):
-        rows = rows_of(group_at(dl, dy) * 2 + flip(x, dx), half_rows)
-        if i == 0:
-            last = place(result.at[rows], attended.at[:, my_columns])
-        else:
-            send(
-                result.at[rows], attended.at[:, my_columns], out_send.at[i], out_recv.at[i],
-                (patch_at(0, dl, dy), flip(x, dx)),
-            )
-    arrive(key_cache.at[rows_of(1 - x, half_rows)], cache_send.at[0], cache_recv.at[0], (patch, 1 - x))
-    for i, (dx, dl, dy) in enumerate(cube):
-        if i > 0:
-            arrive(
-                attended.at[:, columns_of(flip(x, dx) * SPLIT + group_at(dl, dy))],
-                out_send.at[i], out_recv.at[i], (patch_at(0, dl, dy), flip(x, dx)),
-            )
-    last.wait()
+        for i, (dx, dl, dy) in enumerate(cube):
+            if i > 0:
+                arrive(
+                    attended.at[:, head_columns(dx, dl, dy, h)],
+                    out_send.at[h, i], out_recv.at[h, i], (patch_at(0, dl, dy), flip(x, dx)),
+                )
+    for copy in local[-heads:]:
+        copy.wait()
     for copy in started:
         copy.wait_send()
 
@@ -321,9 +335,10 @@
     width = width_dev // SPLIT
     group = (SPLIT * patch_rows, width)
     bf16 = jnp.bfloat16
-    in_vmem = pl.BlockSpec(memory_space=pltpu.VMEM)
-    anywhere = pl.BlockSpec(memory_space=pl.ANY)
-    sems = [(3, 8), (3, 8), (2, 8), (2, 8), (2, 8), (2, 8), (8,), (8,), (1,), (1,), (7,)]
+    in_hbm = pl.BlockSpec(memory_space=pltpu.HBM)
+    sems = [(3, 8), (3, 8), (2, 8), (2, 8), (2, 8), (2, 8)]
+    heads = width // HD
+    sems += [(heads, 8), (heads, 8), (1,), (1,), (10 + heads,)]
     pairs = (width_dev // HD) * patch_rows * tokens
     return pl.pallas_call(
         kernel,
@@ -331,9 +346,12 @@
             jax.ShapeDtypeStruct((half_rows, width_all), bf16),
             jax.ShapeDtypeStruct((patch_rows, width_dev), bf16),
         ],
-        in_specs=[in_vmem, in_vmem, anywhere, anywhere, anywhere, in_vmem, in_vmem],
-        out_specs=[anywhere, anywhere],
+        in_specs=[in_hbm] * 7,
+        out_specs=[in_hbm] * 2,
         scratch_shapes=[
+            pltpu.VMEM((half_rows, width_all), bf16),
+            pltpu.VMEM((half_rows, width_all), bf16),
+            pltpu.VMEM((2, 1, width_all), jnp.float32),
             pltpu.VMEM((half_rows, width_all), bf16),
             pltpu.VMEM((half_rows, width_all), bf16),
             pltpu.VMEM(group, bf16),
@@ -345,7 +363,7 @@
         ]
         + [pltpu.SemaphoreType.DMA(shape) for shape in sems],
         compiler_params=pltpu.CompilerParams(
-            collective_id=0, has_side_effects=True, vmem_limit_bytes=40 * 1024 * 1024
+            collective_id=0, has_side_effects=True, vmem_limit_bytes=62 * 1024 * 1024
         ),
         cost_estimate=pl.CostEstimate(
             flops=4 * pairs * HD, bytes_accessed=8 * tokens * width, transcendentals=pairs

time: 59.1 us -> 52.8 us (0.89)
  local copies, waits for them, and re-layouts: 7.64 us -> 2.46 us
  Pallas kernels: 50.4 us -> 49.5 us
    unnamed x16 -> x4, local copies, waits for them, and re-layouts: 7.64 us -> 2.46 us
    pallas_call x1, Pallas kernels: 50.4 us -> 49.5 us  [kernel_body(): pl.pallas_call(kernel, out_shape=[jax.ShapeDtypeStruct((half_rows, width_...]
where the time goes in v2:
time: 52.8 us; the launch traced here: 52.6 us
  Pallas kernels  49.5 us (94%)
  local copies, waits for them, and re-layouts  2.46 us (5%)
  between operations  0.65 us (1%)
    pallas_call x1, Pallas kernels, kernel_body(): pl.pallas_call(kernel, out_shape=[jax.ShapeDtypeStruct((half_rows, width_...  49.5 us
    unnamed x4, local copies, waits for them, and re-layouts  2.46 us

profile of v2, /device:TPU:0, one launch (start us, length us, event | category | flops | bytes accessed | tf_op | source)
XLA Modules:
  0.0 52.6 jit_solution(12888596196814045443)
XLA Ops:
  0.6 49.5 %shard_map.86 = (bf16[48,3072]{1,0:T(8,128)(2,1)}, bf16[96,1536]{1,0:T(8,128)(2,1)}) custom-call(bf16[48,3072]{1,0:T(8,128)(2,1)} %fresh_q.1, bf16[48,3072]{1,0:T(8,128)(2,1)} %fresh_k.1, bf16[48,3072]{1,0:T(8,128)(2,1)} %fresh_v.1, bf16[96,1536]{1,0:T(8,128)(2,1)} %stale_k.1, bf16[96,1536]{1,0:T(8,128)(2,1)} %stale_v.1, f32[1,3072]{1,0:T(1,128)} %bitcast.2, ...), custom_call_target="tpu_custom_call" | custom-call | flops 905969664 | bytes 4718592 | tf_op jit(solution)/shard_map/pallas_call | solution.py:343
  50.2 0.0 copy-start
  50.2 1.7 %copy.11 = bf16[48,3072]{1,0:T(8,128)(2,1)} copy(bf16[48,3072]{1,0:T(8,128)(2,1)} %get-tuple-element.4) | data formatting | bytes 589824
  51.9 0.0 copy-done
  51.9 0.7 %copy.12 = bf16[96,1536]{1,0:T(8,128)(2,1)} copy(bf16[96,1536]{1,0:T(8,128)(2,1)S(1)} %copy-done) | data formatting | bytes 589824
Async XLA Ops:
  50.2 1.8 %copy-start = (bf16[96,1536]{1,0:T(8,128)(2,1)S(1)}, bf16[96,1536]{1,0:T(8,128)(2,1)}, u32[]{:S(2)}) copy-start(bf16[96,1536]{1,0:T(8,128)(2,1)} %get-tuple-element.5) | copy-start | bytes 884740

commit v3 on v2

--- a/solution.py
+++ b/solution.py
@@ -106,7 +106,7 @@
 def kernel(
     fresh_q, fresh_k, fresh_v, stale_k, stale_v, q_gain, k_gain,
     attended, key_cache,
-    raw_q, raw_k, gains, normed_q, normed_k, q_rows, fresh_k_rows, fresh_v_rows, k_rows, v_rows, result,
+    raw_q, raw_k, gains, own, fresh_rows, stale_rows, result,
     fresh_send, fresh_recv, stale_send, stale_recv, pass_send, pass_recv,
     out_send, out_recv, cache_send, cache_recv, local_sem,
 ):
@@ -172,6 +172,7 @@
         local.append(copy)
         return copy
 
+    place(fresh_v, own.at[2])
     place(fresh_q, raw_q)
     place(fresh_k, raw_k)
     place(q_gain, gains.at[0])
@@ -179,66 +180,57 @@
     pl.semaphore_wait(barrier, len(partners))
 
     my_rows = rows_of(group_at(0, 0) * 2 + x, half_rows)
-    fresh = [(normed_q, q_rows), (normed_k, fresh_k_rows), (fresh_v, fresh_v_rows)]
-    stale = [(stale_k, k_rows), (stale_v, v_rows)]
-
-    def send_fresh(t):
-        source, target = fresh[t]
-        for i, (dx, dl, dy) in enumerate(cube):
-            columns = columns_of(flip(x, dx) * SPLIT + group_at(dl, dy))
+
+    def key_rows_of(high_of, low_of, core_of, y_of):
+        return rows_of(((high_of * 2 + low_of) * 2 + core_of) * 2 + y_of, patch_rows)
+
+    def send_stale(i):
+        dh, dl, dy = plane[i]
+        rows = key_rows_of(high, low, core, y)
+        for t, source in enumerate((stale_k, stale_v)):
+            block = source.at[:, columns_of(group_at(dl, dy))]
             if i == 0:
-                place(source.at[:, columns], target.at[my_rows])
+                place(block, stale_rows.at[t, rows])
             else:
                 send(
-                    source.at[:, columns], target.at[my_rows],
-                    fresh_send.at[t, i], fresh_recv.at[t, i],
-                    (patch_at(0, dl, dy), flip(x, dx)),
-                )
-
-    def send_stale(i):
-        dh, dl, dy = plane[i]
-        rows = rows_of(patch, patch_rows)
-        for t, (source, target) in enumerate(stale):
-            block = source.at[:, columns_of(group_at(dl, dy))]
-            if i == 0:
-                place(block, target.at[rows])
-                send(block, target.at[rows], pass_send.at[t, 0], pass_recv.at[t, 0], sibling)
-            else:
-                send(
-                    block, target.at[rows], stale_send.at[t, i], stale_recv.at[t, i],
+                    block, stale_rows.at[t, rows], stale_send.at[t, i], stale_recv.at[t, i],
                     (patch_at(dh, dl, dy), x),
                 )
 
     for i in range(4, 8):
         send_stale(i)
-    send_fresh(2)
-    for copy in local[:4]:
+    for copy in local[:5]:
         copy.wait()
-    normed_q[...] = rms_rows(raw_q[...], gains[0])
-    send_fresh(0)
-    normed_k[...] = rms_rows(raw_k[...], gains[1])
-    send_fresh(1)
+    own[0] = rms_rows(raw_q[...], gains[0])
+    own[1] = rms_rows(raw_k[...], gains[1])
+    for i, (dx, dl, dy) in enumerate(cube):
+        block = own.at[:, :, columns_of(flip(x, dx) * SPLIT + group_at(dl, dy))]
+        if i == 0:
+            place(block, fresh_rows.at[:, my_rows])
+        else:
+            send(
+                block, fresh_rows.at[:, my_rows], fresh_send.at[i], fresh_recv.at[i],
+                (patch_at(0, dl, dy), flip(x, dx)),
+            )
     for i in range(4):
         send_stale(i)
     cache_rows = rows_of(x, half_rows)
     side = pl.ds(pl.multiple_of(x * width_dev, width_dev), width_dev)
     other_side = pl.ds(pl.multiple_of((1 - x) * width_dev, width_dev), width_dev)
-    place(normed_k.at[:, side], key_cache.at[cache_rows])
+    place(own.at[1, :, side], key_cache.at[cache_rows])
     send(
-        normed_k.at[:, other_side], key_cache.at[cache_rows],
+        own.at[1, :, other_side], key_cache.at[cache_rows],
         cache_send.at[0], cache_recv.at[0], (patch, 1 - x),
     )
-    for copy in local[4:]:
+    for copy in local[5:]:
         copy.wait()
 
-    for t, (_, target) in enumerate(fresh):
-        for i, (dx, dl, dy) in enumerate(cube):
-            if i > 0:
-                arrive(
-                    target.at[rows_of(group_at(dl, dy) * 2 + flip(x, dx), half_rows)],
-                    fresh_send.at[t, i], fresh_recv.at[t, i],
-                    (patch_at(0, dl, dy), flip(x, dx)),
-                )
+    for i, (dx, dl, dy) in enumerate(cube):
+        if i > 0:
+            arrive(
+                fresh_rows.at[:, rows_of(group_at(dl, dy) * 2 + flip(x, dx), half_rows)],
+                fresh_send.at[i], fresh_recv.at[i], (patch_at(0, dl, dy), flip(x, dx)),
+            )
 
     factor = HD ** (-0.5) * 1.4426950408889634
     state = [None] * heads
@@ -248,7 +240,7 @@
     def attend(h, keys, values, masked):
         columns = slice(h * HD, (h + 1) * HD)
         scores = lax.dot_general(
-            q_rows[:, columns], keys[:, columns], (((1,), (1,)), ((), ())),
+            fresh_rows[0, :, columns], keys[:, columns], (((1,), (1,)), ((), ())),
             preferred_element_type=jnp.float32,
         )
         if masked is not None:
@@ -284,36 +276,39 @@
                 )
 
     for h in range(heads):
-        attend(h, fresh_k_rows, fresh_v_rows, row_patch != column_patch)
+        attend(h, fresh_rows.at[1], fresh_rows.at[2], row_patch != column_patch)
 
     for dh, dl in ((1, 0), (1, 1), (0, 0), (0, 1)):
-        indices = [i for i in range(8) if plane[i][:2] == (dh, dl)]
-        for i in indices:
-            rows = rows_of(patch_at(*plane[i]), patch_rows)
-            for t, (_, target) in enumerate(stale):
-                if i > 0:
+        for i in range(8):
+            if i > 0 and plane[i][:2] == (dh, dl):
+                rows = key_rows_of(flip(high, dh), flip(low, dl), core, flip(y, plane[i][2]))
+                for t in range(2):
                     arrive(
-                        target.at[rows], stale_send.at[t, i], stale_recv.at[t, i],
+                        stale_rows.at[t, rows], stale_send.at[t, i], stale_recv.at[t, i],
                         (patch_at(*plane[i]), x),
                     )
-                    send(
-                        target.at[rows], target.at[rows],
-                        pass_send.at[t, i], pass_recv.at[t, i], sibling,
-                    )
-        for i in indices:
-            rows = rows_of(patch_at(*plane[i], 1), patch_rows)
-            for t, (_, target) in enumerate(stale):
-                arrive(target.at[rows], pass_send.at[t, i], pass_recv.at[t, i], sibling)
-        block = rows_of(flip(high, dh) * 2 + flip(low, dl), chunk)
+        step = dh * 2 + dl
+        block = flip(high, dh) * 2 + flip(low, dl)
+        rows = rows_of(block * 2 + core, 2 * patch_rows)
+        send(
+            stale_rows.at[:, rows], stale_rows.at[:, rows],
+            pass_send.at[step], pass_recv.at[step], sibling,
+        )
+        rows = rows_of(block * 2 + 1 - core, 2 * patch_rows)
+        arrive(stale_rows.at[:, rows], pass_send.at[step], pass_recv.at[step], sibling)
+        block = rows_of(block, chunk)
         masked = None
         if dh == 0:
-            key_patch = column_patch + flip(low, dl) * 4
-            masked = row_patch * 2 + core == key_patch
+            row_key = jnp.where(row_patch // 2 == flip(low, dl), row_patch % 2, -1)
+            column_key = jnp.where(column_patch // 2 == core, column_patch % 2, -2)
+            masked = row_key == column_key
         for h in range(heads):
-            attend(h, k_rows.at[block], v_rows.at[block], masked)
+            attend(h, stale_rows.at[0, block], stale_rows.at[1, block], masked)
             if (dh, dl) == (0, 1):
                 give_back(h)
 
+    for copy in started:
+        copy.wait_send()
     arrive(key_cache.at[rows_of(1 - x, half_rows)], cache_send.at[0], cache_recv.at[0], (patch, 1 - x))
     for h in range(heads):
         for i, (dx, dl, dy) in enumerate(cube):
@@ -324,8 +319,6 @@
                 )
     for copy in local[-heads:]:
         copy.wait()
-    for copy in started:
-        copy.wait_send()
 
 
 def kernel_body(fresh_q, fresh_k, fresh_v, stale_k, stale_v, q_gain, k_gain):
@@ -336,9 +329,9 @@
     group = (SPLIT * patch_rows, width)
     bf16 = jnp.bfloat16
     in_hbm = pl.BlockSpec(memory_space=pltpu.HBM)
-    sems = [(3, 8), (3, 8), (2, 8), (2, 8), (2, 8), (2, 8)]
+    sems = [(8,), (8,), (2, 8), (2, 8), (4,), (4,)]
     heads = width // HD
-    sems += [(heads, 8), (heads, 8), (1,), (1,), (10 + heads,)]
+    sems += [(heads, 8), (heads, 8), (1,), (1,), (9 + heads,)]
     pairs = (width_dev // HD) * patch_rows * tokens
     return pl.pallas_call(
         kernel,
@@ -352,13 +345,9 @@
             pltpu.VMEM((half_rows, width_all), bf16),
             pltpu.VMEM((half_rows, width_all), bf16),
             pltpu.VMEM((2, 1, width_all), jnp.float32),
-            pltpu.VMEM((half_rows, width_all), bf16),
-            pltpu.VMEM((half_rows, width_all), bf16),
-            pltpu.VMEM(group, bf16),
-            pltpu.VMEM(group, bf16),
-            pltpu.VMEM(group, bf16),
-            pltpu.VMEM((tokens, width), bf16),
-            pltpu.VMEM((tokens, width), bf16),
+            pltpu.VMEM((3, half_rows, width_all), bf16),
+            pltpu.VMEM((3,) + group, bf16),
+            pltpu.VMEM((2, tokens, width), bf16),
             pltpu.VMEM(group, bf16),
         ]
         + [pltpu.SemaphoreType.DMA(shape) for shape in sems],

time: 52.8 us -> 52.7 us (level)
  no operation moved by 1% of the time
where the time goes in v3:
time: 52.7 us; the launch traced here: 52.6 us
  Pallas kernels  49.5 us (94%)
  local copies, waits for them, and re-layouts  2.46 us (5%)
  between operations  0.65 us (1%)
    pallas_call x1, Pallas kernels, kernel_body(): pl.pallas_call(kernel, out_shape=[jax.ShapeDtypeStruct((half_rows, width_...  49.5 us
    unnamed x4, local copies, waits for them, and re-layouts  2.46 us

profile of v3, /device:TPU:0, one launch (start us, length us, event | category | flops | bytes accessed | tf_op | source)
XLA Modules:
  0.0 52.6 jit_solution(727683231807732815)
XLA Ops:
  0.6 49.5 %shard_map.86 = (bf16[48,3072]{1,0:T(8,128)(2,1)}, bf16[96,1536]{1,0:T(8,128)(2,1)}) custom-call(bf16[48,3072]{1,0:T(8,128)(2,1)} %fresh_q.1, bf16[48,3072]{1,0:T(8,128)(2,1)} %fresh_k.1, bf16[48,3072]{1,0:T(8,128)(2,1)} %fresh_v.1, bf16[96,1536]{1,0:T(8,128)(2,1)} %stale_k.1, bf16[96,1536]{1,0:T(8,128)(2,1)} %stale_v.1, f32[1,3072]{1,0:T(1,128)} %bitcast.2, ...), custom_call_target="tpu_custom_call" | custom-call | flops 905969664 | bytes 4718592 | tf_op jit(solution)/shard_map/pallas_call | solution.py:336
  50.1 0.0 copy-start
  50.1 1.7 %copy.11 = bf16[48,3072]{1,0:T(8,128)(2,1)} copy(bf16[48,3072]{1,0:T(8,128)(2,1)} %get-tuple-element.4) | data formatting | bytes 589824
  51.8 0.0 copy-done
  51.8 0.7 %copy.12 = bf16[96,1536]{1,0:T(8,128)(2,1)} copy(bf16[96,1536]{1,0:T(8,128)(2,1)S(1)} %copy-done) | data formatting | bytes 589824
Async XLA Ops:
  50.1 1.8 %copy-start = (bf16[96,1536]{1,0:T(8,128)(2,1)S(1)}, bf16[96,1536]{1,0:T(8,128)(2,1)}, u32[]{:S(2)}) copy-start(bf16[96,1536]{1,0:T(8,128)(2,1)} %get-tuple-element.5) | copy-start | bytes 884740

commit v4 on v3

--- a/solution.py
+++ b/solution.py
@@ -197,13 +197,8 @@
                     (patch_at(dh, dl, dy), x),
                 )
 
-    for i in range(4, 8):
-        send_stale(i)
-    for copy in local[:5]:
-        copy.wait()
-    own[0] = rms_rows(raw_q[...], gains[0])
-    own[1] = rms_rows(raw_k[...], gains[1])
-    for i, (dx, dl, dy) in enumerate(cube):
+    def send_fresh(i):
+        dx, dl, dy = cube[i]
         block = own.at[:, :, columns_of(flip(x, dx) * SPLIT + group_at(dl, dy))]
         if i == 0:
             place(block, fresh_rows.at[:, my_rows])
@@ -212,8 +207,21 @@
                 block, fresh_rows.at[:, my_rows], fresh_send.at[i], fresh_recv.at[i],
                 (patch_at(0, dl, dy), flip(x, dx)),
             )
-    for i in range(4):
+
+    for i in (4, 2, 5, 3, 1, 0):
         send_stale(i)
+    for copy in local[:5]:
+        copy.wait()
+    own[0] = rms_rows(raw_q[...], gains[0])
+    own[1] = rms_rows(raw_k[...], gains[1])
+    send_fresh(2)
+    send_fresh(3)
+    send_stale(6)
+    send_fresh(6)
+    send_fresh(7)
+    send_stale(7)
+    for i in (1, 4, 5, 0):
+        send_fresh(i)
     cache_rows = rows_of(x, half_rows)
     side = pl.ds(pl.multiple_of(x * width_dev, width_dev), width_dev)
     other_side = pl.ds(pl.multiple_of((1 - x) * width_dev, width_dev), width_dev)
@@ -278,7 +286,7 @@
     for h in range(heads):
         attend(h, fresh_rows.at[1], fresh_rows.at[2], row_patch != column_patch)
 
-    for dh, dl in ((1, 0), (1, 1), (0, 0), (0, 1)):
+    for dh, dl in ((0, 0), (0, 1), (1, 0), (1, 1)):
         for i in range(8):
             if i > 0 and plane[i][:2] == (dh, dl):
                 rows = key_rows_of(flip(high, dh), flip(low, dl), core, flip(y, plane[i][2]))
@@ -304,7 +312,7 @@
             masked = row_key == column_key
         for h in range(heads):
             attend(h, stale_rows.at[0, block], stale_rows.at[1, block], masked)
-            if (dh, dl) == (0, 1):
+            if (dh, dl) == (1, 1):
                 give_back(h)
 
     for copy in started:

time: 52.7 us -> 55.2 us (1.047)
  Pallas kernels: 49.5 us -> 51.9 us
    pallas_call x1, Pallas kernels: 49.5 us -> 51.9 us  [kernel_body(): pl.pallas_call(kernel, out_shape=[jax.ShapeDtypeStruct((half_rows, width_...]
where the time goes in v4:
time: 55.2 us; the launch traced here: 55 us
  Pallas kernels  51.9 us (94%)
  local copies, waits for them, and re-layouts  2.46 us (4%)
  between operations  0.65 us (1%)
    pallas_call x1, Pallas kernels, kernel_body(): pl.pallas_call(kernel, out_shape=[jax.ShapeDtypeStruct((half_rows, width_...  51.9 us
    unnamed x4, local copies, waits for them, and re-layouts  2.46 us

profile of v4, /device:TPU:0, one launch (start us, length us, event | category | flops | bytes accessed | tf_op | source)
XLA Modules:
  0.0 55.0 jit_solution(17600397728710285467)
XLA Ops:
  0.6 51.9 %shard_map.86 = (bf16[48,3072]{1,0:T(8,128)(2,1)}, bf16[96,1536]{1,0:T(8,128)(2,1)}) custom-call(bf16[48,3072]{1,0:T(8,128)(2,1)} %fresh_q.1, bf16[48,3072]{1,0:T(8,128)(2,1)} %fresh_k.1, bf16[48,3072]{1,0:T(8,128)(2,1)} %fresh_v.1, bf16[96,1536]{1,0:T(8,128)(2,1)} %stale_k.1, bf16[96,1536]{1,0:T(8,128)(2,1)} %stale_v.1, f32[1,3072]{1,0:T(1,128)} %bitcast.2, ...), custom_call_target="tpu_custom_call" | custom-call | flops 905969664 | bytes 4718592 | tf_op jit(solution)/shard_map/pallas_call | solution.py:344
  52.5 0.0 copy-start
  52.5 1.7 %copy.11 = bf16[48,3072]{1,0:T(8,128)(2,1)} copy(bf16[48,3072]{1,0:T(8,128)(2,1)} %get-tuple-element.4) | data formatting | bytes 589824
  54.3 0.0 copy-done
  54.3 0.7 %copy.12 = bf16[96,1536]{1,0:T(8,128)(2,1)} copy(bf16[96,1536]{1,0:T(8,128)(2,1)S(1)} %copy-done) | data formatting | bytes 589824
Async XLA Ops:
  52.5 1.8 %copy-start = (bf16[96,1536]{1,0:T(8,128)(2,1)S(1)}, bf16[96,1536]{1,0:T(8,128)(2,1)}, u32[]{:S(2)}) copy-start(bf16[96,1536]{1,0:T(8,128)(2,1)} %get-tuple-element.5) | copy-start | bytes 884740

commit v5 on v3

--- a/solution.py
+++ b/solution.py
@@ -152,12 +152,13 @@
 
     started, local = [], []
 
-    def send(source, target, send_sem, recv_sem, device):
+    def send(source, target, send_sem, recv_sem, device, now=True):
         copy = pltpu.make_async_remote_copy(
             src_ref=source, dst_ref=target, send_sem=send_sem, recv_sem=recv_sem,
             device_id=device, device_id_type=MESH_TYPE,
         )
-        copy.start()
+        if now:
+            copy.start()
         started.append(copy)
 
     def arrive(target, send_sem, recv_sem, device):
@@ -194,11 +195,18 @@
             else:
                 send(
                     block, stale_rows.at[t, rows], stale_send.at[t, i], stale_recv.at[t, i],
-                    (patch_at(dh, dl, dy), x),
+                    (patch_at(dh, dl, dy), x), now=dh == 0,
                 )
 
     for i in range(4, 8):
         send_stale(i)
+    far = list(started)
+
+    @pl.when(low != high)
+    def _():
+        for copy in far:
+            copy.start()
+
     for copy in local[:5]:
         copy.wait()
     own[0] = rms_rows(raw_q[...], gains[0])
@@ -214,6 +222,12 @@
             )
     for i in range(4):
         send_stale(i)
+
+    @pl.when(low == high)
+    def _():
+        for copy in far:
+            copy.start()
+
     cache_rows = rows_of(x, half_rows)
     side = pl.ds(pl.multiple_of(x * width_dev, width_dev), width_dev)
     other_side = pl.ds(pl.multiple_of((1 - x) * width_dev, width_dev), width_dev)
@@ -278,7 +292,7 @@
     for h in range(heads):
         attend(h, fresh_rows.at[1], fresh_rows.at[2], row_patch != column_patch)
 
-    for dh, dl in ((1, 0), (1, 1), (0, 0), (0, 1)):
+    for dh, dl in ((0, 0), (0, 1), (1, 0), (1, 1)):
         for i in range(8):
             if i > 0 and plane[i][:2] == (dh, dl):
                 rows = key_rows_of(flip(high, dh), flip(low, dl), core, flip(y, plane[i][2]))
@@ -304,7 +318,7 @@
             masked = row_key == column_key
         for h in range(heads):
             attend(h, stale_rows.at[0, block], stale_rows.at[1, block], masked)
-            if (dh, dl) == (0, 1):
+            if (dh, dl) == (1, 1):
                 give_back(h)
 
     for copy in started:

time: 52.7 us -> 47.3 us (0.90)
  Pallas kernels: 49.5 us -> 43.8 us
    pallas_call x1, Pallas kernels: 49.5 us -> 43.8 us  [kernel_body(): pl.pallas_call(kernel, out_shape=[jax.ShapeDtypeStruct((half_rows, width_...]
where the time goes in v5:
time: 47.3 us; the launch traced here: 46.9 us
  Pallas kernels  43.8 us (93%)
  local copies, waits for them, and re-layouts  2.46 us (5%)
  between operations  0.65 us (1%)
    pallas_call x1, Pallas kernels, kernel_body(): pl.pallas_call(kernel, out_shape=[jax.ShapeDtypeStruct((half_rows, width_...  43.8 us
    unnamed x4, local copies, waits for them, and re-layouts  2.46 us

profile of v5, /device:TPU:0, one launch (start us, length us, event | category | flops | bytes accessed | tf_op | source)
XLA Modules:
  0.0 46.9 jit_solution(2262037410683177636)
XLA Ops:
  0.6 43.8 %shard_map.86 = (bf16[48,3072]{1,0:T(8,128)(2,1)}, bf16[96,1536]{1,0:T(8,128)(2,1)}) custom-call(bf16[48,3072]{1,0:T(8,128)(2,1)} %fresh_q.1, bf16[48,3072]{1,0:T(8,128)(2,1)} %fresh_k.1, bf16[48,3072]{1,0:T(8,128)(2,1)} %fresh_v.1, bf16[96,1536]{1,0:T(8,128)(2,1)} %stale_k.1, bf16[96,1536]{1,0:T(8,128)(2,1)} %stale_v.1, f32[1,3072]{1,0:T(1,128)} %bitcast.2, ...), custom_call_target="tpu_custom_call" | custom-call | flops 905969664 | bytes 4718592 | tf_op jit(solution)/shard_map/pallas_call | solution.py:350
  44.4 0.0 copy-start
  44.4 1.7 %copy.11 = bf16[48,3072]{1,0:T(8,128)(2,1)} copy(bf16[48,3072]{1,0:T(8,128)(2,1)} %get-tuple-element.4) | data formatting | bytes 589824
  46.2 0.0 copy-done
  46.2 0.7 %copy.12 = bf16[96,1536]{1,0:T(8,128)(2,1)} copy(bf16[96,1536]{1,0:T(8,128)(2,1)S(1)} %copy-done) | data formatting | bytes 589824
Async XLA Ops:
  44.4 1.8 %copy-start = (bf16[96,1536]{1,0:T(8,128)(2,1)S(1)}, bf16[96,1536]{1,0:T(8,128)(2,1)}, u32[]{:S(2)}) copy-start(bf16[96,1536]{1,0:T(8,128)(2,1)} %get-tuple-element.5) | copy-start | bytes 884740

commit v6 on v5

--- a/solution.py
+++ b/solution.py
@@ -207,6 +207,8 @@
         for copy in far:
             copy.start()
 
+    for i in range(4):
+        send_stale(i)
     for copy in local[:5]:
         copy.wait()
     own[0] = rms_rows(raw_q[...], gains[0])
@@ -220,8 +222,6 @@
                 block, fresh_rows.at[:, my_rows], fresh_send.at[i], fresh_recv.at[i],
                 (patch_at(0, dl, dy), flip(x, dx)),
             )
-    for i in range(4):
-        send_stale(i)
 
     @pl.when(low == high)
     def _():

time: 47.3 us -> 50.7 us (1.072)
  Pallas kernels: 43.8 us -> 47.4 us
    pallas_call x1, Pallas kernels: 43.8 us -> 47.4 us  [kernel_body(): pl.pallas_call(kernel, out_shape=[jax.ShapeDtypeStruct((half_rows, width_...]
where the time goes in v6:
time: 50.7 us; the launch traced here: 50.5 us
  Pallas kernels  47.4 us (93%)
  local copies, waits for them, and re-layouts  2.46 us (5%)
  between operations  0.65 us (1%)
    pallas_call x1, Pallas kernels, kernel_body(): pl.pallas_call(kernel, out_shape=[jax.ShapeDtypeStruct((half_rows, width_...  47.4 us
    unnamed x4, local copies, waits for them, and re-layouts  2.46 us

profile of v6, /device:TPU:0, one launch (start us, length us, event | category | flops | bytes accessed | tf_op | source)
XLA Modules:
  0.0 50.5 jit_solution(2155657057294323162)
XLA Ops:
  0.6 47.4 %shard_map.86 = (bf16[48,3072]{1,0:T(8,128)(2,1)}, bf16[96,1536]{1,0:T(8,128)(2,1)}) custom-call(bf16[48,3072]{1,0:T(8,128)(2,1)} %fresh_q.1, bf16[48,3072]{1,0:T(8,128)(2,1)} %fresh_k.1, bf16[48,3072]{1,0:T(8,128)(2,1)} %fresh_v.1, bf16[96,1536]{1,0:T(8,128)(2,1)} %stale_k.1, bf16[96,1536]{1,0:T(8,128)(2,1)} %stale_v.1, f32[1,3072]{1,0:T(1,128)} %bitcast.2, ...), custom_call_target="tpu_custom_call" | custom-call | flops 905969664 | bytes 4718592 | tf_op jit(solution)/shard_map/pallas_call | solution.py:350
  48.0 0.0 copy-start
  48.0 1.7 %copy.11 = bf16[48,3072]{1,0:T(8,128)(2,1)} copy(bf16[48,3072]{1,0:T(8,128)(2,1)} %get-tuple-element.4) | data formatting | bytes 589824
  49.8 0.0 copy-done
  49.8 0.7 %copy.12 = bf16[96,1536]{1,0:T(8,128)(2,1)} copy(bf16[96,1536]{1,0:T(8,128)(2,1)S(1)} %copy-done) | data formatting | bytes 589824
Async XLA Ops:
  48.0 1.8 %copy-start = (bf16[96,1536]{1,0:T(8,128)(2,1)S(1)}, bf16[96,1536]{1,0:T(8,128)(2,1)}, u32[]{:S(2)}) copy-start(bf16[96,1536]{1,0:T(8,128)(2,1)} %get-tuple-element.5) | copy-start | bytes 884740
